TPU v7x, 32 devices: a whole 2x2x4 slice. The times are simulated.
32 devices in a mesh: orient: 32 (over z, y, x, core), slab: 1.
Axes of the slice: x: 2, y: 2, z: 4, core: 2. Of those that a mesh axis runs over, the one named last changes fastest.
Arguments:
- volume: bfloat16 [32, 128, 8192], P('orient', 'slab'), may hold values from 0 to 2
- rays: bfloat16 [8192, 8, 128], replicated, may hold values from -0.0234375 to 0.0234375
- band_start: int32 [8, 32], P(None, 'orient'), may hold values from 0 to 63
- band_len: int32 [8, 32], P(None, 'orient'), may hold values from 32 to 64
- slot_image: int32 [32], replicated, may hold values from 0 to 31, each once
- measured: float32 [32, 128, 128], P('orient', 'slab'), may hold values from -6 to 6
- relax: float32 [32], P('orient'), may hold values from 0.25 to 1
Outputs:
- updated: bfloat16 [32, 128, 8192], P('orient', 'slab')
- residual: float32 [32, 128, 128], P('orient', 'slab')
Inputs may be any that keep to these rules, and one draw needn't show every extreme that they name: `slot_image`: every image number appears in exactly one slot. band_start + band_len stays below 128.
All inputs are finite; a program needn't handle non-finite values.
Results may differ from a plain program's by a relative error of at most 0.0055.
Values may be sent and summed in bfloat16 or wider, within the bound.
A program may use at most 128 MiB of HBM per device.

v0:
```python
import math

import jax
import jax.numpy as jnp
from jax import lax
from jax.sharding import PartitionSpec as P

FRAMES = 4
SWEEPS = 2


huber_delta = 0.5
sweep_rate = 0.2


def extended_2(cells, sides, width):
    for axis, dim in sides:
        count = lax.axis_size(axis)
        ends = count - 1
        head = lax.slice_in_dim(cells, 0, width, axis=dim)
        tail = lax.slice_in_dim(cells, cells.shape[dim] - width, cells.shape[dim], axis=dim)
        cells = jnp.concatenate(
            [
                lax.ppermute(tail, axis, [(i, (i + 1) % count) for i in range(ends)]),
                cells,
                lax.ppermute(head, axis, [((i + 1) % count, i) for i in range(ends)]),
            ],
            axis=dim,
        )
    return cells


def smooth_pass(extended, first_row, total_rows):
    middle = extended[:, 1:-1]
    row_count = middle.shape[1]
    global_rows = first_row + 1 + jnp.arange(row_count, dtype=jnp.int32)
    has_above = (global_rows > 0)[None, :, None]
    has_below = (global_rows < total_rows - 1)[None, :, None]
    from_above = jnp.clip(middle - extended[:, :-2], -huber_delta, huber_delta)
    from_below = jnp.clip(middle - extended[:, 2:], -huber_delta, huber_delta)
    row_flux = jnp.where(has_above, from_above, 0.0) + jnp.where(has_below, from_below, 0.0)
    return middle - sweep_rate * row_flux


def local(volume, rays, band_start, band_len, slot_image, measured, relax):
    or_dev, row_dev, cell_count = volume.shape
    reflections_n, detector = (rays.shape[1], rays.shape[2])
    images_n = reflections_n * FRAMES
    orient_groups = lax.axis_size("orient")
    orients_all = or_dev * orient_groups
    reflections = jnp.arange(reflections_n, dtype=jnp.int32)
    columns = jnp.arange(detector, dtype=jnp.int32)
    inside = (columns >= band_start[:, :, None]) & (columns < (band_start + band_len)[:, :, None])
    band_mask = inside.astype(jnp.float32)
    inverse = (
        jnp.zeros((images_n,), jnp.int32).at[slot_image].set(jnp.arange(images_n, dtype=jnp.int32))
    )
    flat_rays = rays.reshape(cell_count, reflections_n * detector)
    projected = jnp.dot(
        volume.reshape(or_dev * row_dev, cell_count), flat_rays, preferred_element_type=jnp.float32
    )
    projected = projected.reshape(or_dev, row_dev, reflections_n, detector)
    pixels = row_dev * detector
    contrib = jnp.einsum("kod,orkd->okrd", band_mask, projected).reshape(
        or_dev, reflections_n, pixels
    )
    parts = lax.all_to_all(contrib, "orient", split_axis=2, concat_axis=0, tiled=True)
    every_orient = jnp.arange(orients_all, dtype=jnp.int32)
    frame_all = (every_orient[:, None] + reflections[None, :]) % FRAMES
    pick_all = (frame_all[:, :, None] == jnp.arange(FRAMES, dtype=jnp.int32)).astype(jnp.float32)
    summed = jnp.einsum("okf,okp->kfp", pick_all, parts).reshape(images_n, parts.shape[2])
    owned = lax.all_to_all(summed[slot_image], "orient", split_axis=0, concat_axis=1, tiled=True)
    residual = measured - owned.reshape(measured.shape)
    sent = residual.astype(jnp.bfloat16).reshape(measured.shape[0], pixels)
    shares = lax.all_to_all(sent, "orient", split_axis=1, concat_axis=0, tiled=True)
    share_image = shares[inverse]
    selected = share_image[reflections[None, :] * FRAMES + frame_all]
    mine = lax.all_to_all(selected, "orient", split_axis=0, concat_axis=2, tiled=True)
    picked = mine.reshape(or_dev, reflections_n, row_dev, detector)
    masked = picked * jnp.transpose(band_mask, (1, 0, 2))[:, :, None, :].astype(jnp.bfloat16)
    gradient = jnp.einsum("okrd,ckd->orc", masked, rays, preferred_element_type=jnp.float32)
    step_gain = math.sqrt(cell_count * orients_all / (FRAMES * reflections_n * detector))
    density = volume.astype(jnp.float32) + relax[:, None, None] * step_gain * gradient
    total_rows = row_dev * lax.axis_size("slab")
    base_row = lax.axis_index("slab") * row_dev
    for repeat in range(SWEEPS):
        extended = extended_2(density, (("slab", 1),), 1)
        density = smooth_pass(extended, base_row - 1, total_rows)
    return (density.astype(jnp.bfloat16), residual)


def solution(mesh):
    placed = (
        P("orient", "slab", None),
        P(),
        P(None, "orient"),
        P(None, "orient"),
        P(),
        P("orient", "slab", None),
        P("orient"),
    )
    return jax.shard_map(
        local,
        mesh=mesh,
        in_specs=placed,
        out_specs=(P("orient", "slab", None), P("orient", "slab", None)),
        check_vma=False,
    )
```

profile of v0, /device:TPU:9, one launch (start us, length us, event | category | flops | bytes accessed | tf_op | source)
XLA Modules:
  0.0 251.3 jit_solution(3620101442549288618)
XLA Ops:
  0.6 15.6 %copy.54 = bf16[1024,8,8,128]{3,1,2,0:T(8,128)(2,1)} copy(bf16[1024,8,8,128]{3,2,1,0:T(8,128)(2,1)} %bitcast.66) | data formatting | bytes 33554432
  16.2 0.0 copy-start.1
  16.2 0.0 copy-start.3
  16.2 0.0 copy-start.2
  16.2 21.5 %copy.31 = bf16[1024,8192]{1,0:T(8,128)(2,1)} copy(bf16[1024,8192]{0,1:T(8,128)(2,1)} %bitcast.63) | data formatting | bytes 33554432 | tf_op jit(solution)/shard_map/dot_general | solution.py:59
  37.8 0.0 copy-done.1
  37.8 0.0 copy-done.3
  37.8 0.1 fusion.57
  37.9 0.0 copy-done.2
  37.9 8.4 %fusion.38 = f32[1,8,128,128]{2,3,1,0:T(8,128)S(1)} fusion(bf16[8,128,8192]{2,1,0:T(8,128)(2,1)} %bitcast.67, bf16[1,128,8192]{2,1,0:T(8,128)(2,1)S(1)} %copy-done.2, f32[8,128]{1,0:T(8,128)S(1)} %get-tuple-element.9), kind=kOutput, calls=%fused_computation.37 | convolution fusion | flops 2147614720 | bytes 19402752 | tf_op jit(solution)/shard_map/dot_general | solution.py:59
  46.2 0.2 copy.32
  46.4 11.9 %copy.33 = f32[1,8,16384]{1,0,2:T(1,128)} copy(f32[1,8,16384]{2,0,1:T(1,128)S(1)} %bitcast.69) | data formatting | bytes 1048576 | tf_op jit(solution)/shard_map/reshape | solution.py:64
  58.3 0.5 broadcast.199
  58.8 74.5 %reduce = f32[16384,8]{1,0:T(8,128)} reduce(f32[16384,1,8]{2,1,0:T(1,128)} %bitcast.64, f32[]{:T(128)} %broadcast.199), dimensions={1}, to_apply=%bitcast.54.reduce_sub_computation | reduce | bytes 1048580
  133.3 0.0 copy-start.4
  133.3 7.3 %reshape.295 = f32[32,1,4096]{2,1,0:T(1,128)} reshape(f32[16384,8]{1,0:T(8,128)} %reduce) | data formatting | bytes 1048576
  140.6 6.4 %all-to-all-start = ((f32[32,1,4096]{2,1,0:T(1,128)}), f32[32,1,4096]{2,1,0:T(1,128)S(1)}, u32[]{:S(2)}, u32[]{:S(2)}) async-start(f32[32,1,4096]{2,1,0:T(1,128)} %reshape.295), calls=%async_computation | async-start | bytes 1048576 | tf_op jit(solution)/shard_map/all_to_all | solution.py:67
  147.0 0.0 copy-done.4
  147.0 0.9 scatter_custom_fusion
  148.0 13.3 %all-to-all-done = f32[32,1,4096]{2,1,0:T(1,128)S(1)} async-done(((f32[32,1,4096]{2,1,0:T(1,128)}), f32[32,1,4096]{2,1,0:T(1,128)S(1)}, u32[]{:S(2)}, u32[]{:S(2)}) %all-to-all-start) | async-done | bytes 524320 | tf_op jit(solution)/shard_map/all_to_all | solution.py:67
  161.2 1.9 reduce.1
  163.1 15.4 %reshape.296 = f32[16384,1,8]{2,1,0:T(1,128)} reshape(f32[32,4096]{1,0:T(8,128)S(1)} %reduce.1) | data formatting | bytes 1048576
  178.6 0.0 copy-start
  178.6 5.2 %copy.39 = bf16[1,8,32,512]{3,2,1,0:T(8,128)(2,1)S(1)} copy(f32[1,8,32,512]{1,3,2,0:T(8,128)} %bitcast.65) | data formatting | bytes 786432 | tf_op jit(solution)/shard_map/all_to_all | solution.py:67
  183.8 0.1 fusion.41
  183.9 0.6 gather_fusion
  184.6 0.7 copy.35
  185.2 4.4 %all-to-all-start.1 = ((f32[32,1,512]{2,1,0:T(1,128)}), f32[32,1,512]{2,1,0:T(1,128)S(1)}, u32[]{:S(2)}, u32[]{:S(2)}) async-start(f32[32,1,512]{2,1,0:T(1,128)} %copy.35), calls=%async_computation.1 | async-start | bytes 131072 | tf_op jit(solution)/shard_map/all_to_all | solution.py:72
  189.7 0.1 reshape.273
  189.8 5.5 %all-to-all-done.1 = f32[32,1,512]{2,1,0:T(1,128)S(1)} async-done(((f32[32,1,512]{2,1,0:T(1,128)}), f32[32,1,512]{2,1,0:T(1,128)S(1)}, u32[]{:S(2)}, u32[]{:S(2)}) %all-to-all-start.1) | async-done | bytes 65568 | tf_op jit(solution)/shard_map/all_to_all | solution.py:72
  195.3 0.0 copy-done
  195.3 0.6 fusion.60
  195.9 0.5 broadcast.201
  196.4 0.8 reduce.2
  197.3 0.6 reshape.297
  197.9 4.3 %all-to-all-start.2 = ((bf16[32,2,256]{2,1,0:T(2,128)(2,1)}), bf16[32,2,256]{2,1,0:T(2,128)(2,1)S(1)}, u32[]{:S(2)}, u32[]{:S(2)}) async-start(bf16[32,2,256]{2,1,0:T(2,128)(2,1)} %reshape.297), calls=%async_computation.2 | async-start | bytes 65536 | tf_op jit(solution)/shard_map/all_to_all | solution.py:75
  202.2 5.6 %all-to-all-done.2 = bf16[32,2,256]{2,1,0:T(2,128)(2,1)S(1)} async-done(((bf16[32,2,256]{2,1,0:T(2,128)(2,1)}), bf16[32,2,256]{2,1,0:T(2,128)(2,1)S(1)}, u32[]{:S(2)}, u32[]{:S(2)}) %all-to-all-start.2) | async-done | bytes 32800 | tf_op jit(solution)/shard_map/all_to_all | solution.py:75
  207.9 0.6 gather_fusion.1
  208.5 1.9 gather_fusion.2
  210.4 4.2 %all-to-all-start.3 = ((bf16[32,8,512]{2,1,0:T(8,128)(2,1)}), bf16[32,8,512]{2,1,0:T(8,128)(2,1)S(1)}, u32[]{:S(2)}, u32[]{:S(2)}) async-start(bf16[32,8,512]{2,1,0:T(8,128)(2,1)} %bitcast.15), calls=%async_computation.3 | async-start | bytes 524288 | tf_op jit(solution)/shard_map/all_to_all | solution.py:78
  215.2 8.1 %all-to-all-done.3 = bf16[32,8,512]{2,1,0:T(8,128)(2,1)S(1)} async-done(((bf16[32,8,512]{2,1,0:T(8,128)(2,1)}), bf16[32,8,512]{2,1,0:T(8,128)(2,1)S(1)}, u32[]{:S(2)}, u32[]{:S(2)}) %all-to-all-start.3) | async-done | bytes 262176 | tf_op jit(solution)/shard_map/all_to_all | solution.py:78
  223.3 0.1 copy.37
  223.4 0.2 reshape.254
  223.6 13.4 %fusion.11 = f32[1,128,8192]{2,1,0:T(8,128)} fusion(bf16[8192,8,128]{2,1,0:T(8,128)(2,1)} %param.8, bf16[1,128,8192]{2,1,0:T(8,128)(2,1)S(1)} %copy-done.2, f32[]{:T(128)} %bitcast, bf16[8,128,128]{2,1,0:T(8,128)(2,1)S(1)} %reshape.254, bf16[8,128]{1,0:T(8,128)(2,1)S(1)} %get-tuple-element.8), kind=kOutput, calls=%fused_computation.10 | convolution fusion | flops 2150760448 | bytes 23332868 | tf_op jit(solution)/shard_map/okrd,ckd->orc/dot_general | solution.py:81
  237.0 1.1 fusion.62
  238.1 0.7 collective-permute-start.1
  238.7 0.9 collective-permute-start
  239.6 0.0 collective-permute-done.1
  239.6 0.0 collective-permute-done
  239.7 6.1 %fusion.29 = f32[1,128,8192]{2,1,0:T(8,128)S(1)} fusion(f32[1,128,8192]{2,1,0:T(8,128)} %fusion.11, f32[1,1,8192]{2,1,0:T(1,128)S(1)} %collective-permute-done.1, f32[1,1,8192]{2,1,0:T(1,128)S(1)} %collective-permute-done, pred[128]{0:T(512)(128)(4,1)S(1)} %get-tuple-element.10, pred[128]{0:T(512)(128)(4,1)S(1)} %get-tuple-element.11), kind=kLoop, calls=%fused_computation.29 | loop fusion | flops 11534336 | bytes 8454400 | tf_op jit(solution)/shard_map/sub | solution.py:42
  245.8 0.7 collective-permute-start.3
  246.5 0.7 collective-permute-start.2
  247.1 0.0 collective-permute-done.3
  247.1 0.0 collective-permute-done.2
  247.1 4.2 %fusion.20 = bf16[1,128,8192]{2,1,0:T(8,128)(2,1)} fusion(f32[1,128,8192]{2,1,0:T(8,128)S(1)} %fusion.29, f32[1,1,8192]{2,1,0:T(1,128)S(1)} %collective-permute-done.3, f32[1,1,8192]{2,1,0:T(1,128)S(1)} %collective-permute-done.2, pred[128]{0:T(512)(128)(4,1)S(1)} %get-tuple-element.10, pred[128]{0:T(512)(128)(4,1)S(1)} %get-tuple-element.11), kind=kLoop, calls=%fused_computation.18 | loop fusion | flops 12582912 | bytes 6357248 | tf_op jit(solution)/shard_map/convert_element_type | solution.py:89
  (16 shorter events, 0.2 us)
Async XLA Ops:
  16.2 21.5 %copy-start.1 = (s32[8,1]{0,1:T(1,128)S(1)}, s32[8,1]{0,1:T(1,128)}, u32[]{:S(2)}) copy-start(s32[8,1]{0,1:T(1,128)} %param.9) | copy-start | bytes 100
  16.2 21.5 %copy-start.3 = (s32[8,1]{0,1:T(1,128)S(1)}, s32[8,1]{0,1:T(1,128)}, u32[]{:S(2)}) copy-start(s32[8,1]{0,1:T(1,128)} %param.10) | copy-start | bytes 100
  16.2 21.6 %copy-start.2 = (bf16[1,128,8192]{2,1,0:T(8,128)(2,1)S(1)}, bf16[1,128,8192]{2,1,0:T(8,128)(2,1)}, u32[]{:S(2)}) copy-start(bf16[1,128,8192]{2,1,0:T(8,128)(2,1)} %param.7) | copy-start | bytes 6291460
  133.3 13.7 %copy-start.4 = (s32[32]{0:T(128)S(1)}, s32[32]{0:T(128)}, u32[]{:S(2)}) copy-start(s32[32]{0:T(128)} %param.11) | copy-start | bytes 388
  140.6 20.6 %all-to-all-start = ((f32[32,1,4096]{2,1,0:T(1,128)}), f32[32,1,4096]{2,1,0:T(1,128)S(1)}, u32[]{:S(2)}, u32[]{:S(2)}) async-start(f32[32,1,4096]{2,1,0:T(1,128)} %reshape.295), calls=%async_computation | async-start | bytes 1048576 | tf_op jit(solution)/shard_map/all_to_all | solution.py:67
  178.6 16.7 %copy-start = (f32[1,128,128]{2,1,0:T(8,128)S(1)}, f32[1,128,128]{2,1,0:T(8,128)}, u32[]{:S(2)}) copy-start(f32[1,128,128]{2,1,0:T(8,128)} %param.12) | copy-start | bytes 196612
  185.2 10.0 %all-to-all-start.1 = ((f32[32,1,512]{2,1,0:T(1,128)}), f32[32,1,512]{2,1,0:T(1,128)S(1)}, u32[]{:S(2)}, u32[]{:S(2)}) async-start(f32[32,1,512]{2,1,0:T(1,128)} %copy.35), calls=%async_computation.1 | async-start | bytes 131072 | tf_op jit(solution)/shard_map/all_to_all | solution.py:72
  197.9 10.0 %all-to-all-start.2 = ((bf16[32,2,256]{2,1,0:T(2,128)(2,1)}), bf16[32,2,256]{2,1,0:T(2,128)(2,1)S(1)}, u32[]{:S(2)}, u32[]{:S(2)}) async-start(bf16[32,2,256]{2,1,0:T(2,128)(2,1)} %reshape.297), calls=%async_computation.2 | async-start | bytes 65536 | tf_op jit(solution)/shard_map/all_to_all | solution.py:75
  210.4 12.9 %all-to-all-start.3 = ((bf16[32,8,512]{2,1,0:T(8,128)(2,1)}), bf16[32,8,512]{2,1,0:T(8,128)(2,1)S(1)}, u32[]{:S(2)}, u32[]{:S(2)}) async-start(bf16[32,8,512]{2,1,0:T(8,128)(2,1)} %bitcast.15), calls=%async_computation.3 | async-start | bytes 524288 | tf_op jit(solution)/shard_map/all_to_all | solution.py:78
  238.1 1.6 collective-permute-start.1
  238.7 0.9 collective-permute-start
  245.8 1.3 collective-permute-start.3
  246.5 0.7 collective-permute-start.2
where the time goes:
time: 255 us; the launch traced here: 251 us
  other arithmetic  88.2 us (35%)
  local copies, waits for them, and re-layouts  85 us (33%)
  waiting for transfers between devices  32.5 us (13%)
  starting transfers between devices  22.1 us (9%)
  matrix products  21.9 us (9%)
    unnamed x2, other arithmetic  75.3 us
    unnamed x18, local copies, waits for them, and re-layouts  40.1 us
    dot_general x1, local copies, waits for them, and re-layouts, local(): jnp.dot(volume.reshape(or_dev * row_dev, cell_count), flat_rays, preferre...  21.5 us
    dot_general x1, matrix products, local(): jnp.einsum('okrd,ckd->orc', masked, rays, preferred_element_type=jnp.floa...  13.4 us
    all_to_all x1, waiting for transfers between devices, local(): lax.all_to_all(contrib, 'orient', split_axis=2, concat_axis=0, tiled=True)  13.3 us
    reshape x1, local copies, waits for them, and re-layouts, local(): jnp.einsum('kod,orkd->okrd', band_mask, projected)  11.9 us
    dot_general x1, matrix products, local(): jnp.dot(volume.reshape(or_dev * row_dev, cell_count), flat_rays, preferre...  8.35 us
    all_to_all x1, waiting for transfers between devices, local(): lax.all_to_all(selected, 'orient', split_axis=0, concat_axis=2, tiled=True)  8.11 us
  transfers between devices with their start and end apart: 8, of which 4 were waited for; matrix products, arithmetic and copies ran while one was open for 0% of the time, Pallas kernels for 0%

commit v1 on v0

--- a/solution.py
+++ b/solution.py
@@ -3,6 +3,8 @@
 import jax
 import jax.numpy as jnp
 from jax import lax
+from jax.experimental import pallas as pl
+from jax.experimental.pallas import tpu as pltpu
 from jax.sharding import PartitionSpec as P
 
 FRAMES = 4
@@ -89,6 +91,269 @@
     return (density.astype(jnp.bfloat16), residual)
 
 
+def band(start_ref, len_ref, k, shape):
+    column = lax.broadcasted_iota(jnp.int32, shape, len(shape) - 1)
+    first = start_ref[k, 0]
+    return (column >= first) & (column < first + len_ref[k, 0])
+
+
+def forward_kernel(start_ref, len_ref, volume_ref, rays_ref, flat_ref, contrib_ref, wide, total):
+    step = pl.program_id(0)
+    cells, reflections_n, detector = rays_ref.shape
+    members, _, share, _ = contrib_ref.shape
+
+    @pl.when(step == 0)
+    def _():
+        total[...] = jnp.zeros_like(total)
+
+    wide[...] = rays_ref[...].astype(jnp.float32).reshape(cells * reflections_n, detector)
+    for k in range(reflections_n):
+        part = wide[pl.ds(k, cells, stride=reflections_n), :]
+        flat_ref[:, k * detector:(k + 1) * detector] = part.astype(jnp.bfloat16)
+    total[...] += jnp.dot(volume_ref[...], flat_ref[...], preferred_element_type=jnp.float32)
+
+    @pl.when(step == pl.num_programs(0) - 1)
+    def _():
+        for k in range(reflections_n):
+            inside = band(start_ref, len_ref, k, (share, detector))
+            for i in range(members):
+                block = total[i * share:(i + 1) * share, k * detector:(k + 1) * detector]
+                contrib_ref[i, k] = jnp.where(inside, block, 0.0).astype(jnp.bfloat16)
+
+
+def exchange_kernel(
+    n, start_ref, len_ref, slot_ref, inverse_ref, contrib_ref, measured_ref, masked_ref, residual_ref,
+    pieces, images, gathered, outgoing, incoming,
+    image_send, image_recv, piece_send, piece_recv, gather_send, gather_recv, quad_send, quad_recv,
+):
+    members, reflections_n, share, detector = contrib_ref.shape
+    me = lax.axis_index("orient")
+    group = lax.rem(me, FRAMES)
+    member = me // FRAMES
+
+    def remote(source, target, send, recv, device):
+        return pltpu.make_async_remote_copy(
+            src_ref=source, dst_ref=target, send_sem=send, recv_sem=recv,
+            device_id={"orient": device}, device_id_type=pl.DeviceIdType.MESH,
+        )
+
+    barrier = pltpu.get_barrier_semaphore()
+
+    @pl.loop(1, n)
+    def _(s):
+        pl.semaphore_signal(
+            barrier, inc=1, device_id={"orient": lax.rem(me + s, n)},
+            device_id_type=pl.DeviceIdType.MESH,
+        )
+
+    pl.semaphore_wait(barrier, n - 1)
+
+    def piece_copy(s):
+        other = lax.rem(member + s, members)
+        return remote(
+            contrib_ref.at[other], pieces.at[s - 1], piece_send.at[s - 1], piece_recv.at[s - 1],
+            other * FRAMES + group,
+        )
+
+    def image_copy(s):
+        device = lax.rem(me + s, n)
+        return remote(
+            measured_ref.at[device // FRAMES], images.at[s], image_send.at[s], image_recv.at[s], device
+        )
+
+    for s in range(1, members):
+        piece_copy(s).start()
+
+    @pl.loop(1, n)
+    def _(s):
+        image_copy(s).start()
+
+    images[0] = measured_ref[member]
+    total = contrib_ref[member].astype(jnp.float32)
+    for s in range(1, members):
+        piece_copy(s).wait()
+        total = total + pieces[s - 1].astype(jnp.float32)
+
+    @pl.loop(1, n)
+    def _(s):
+        image_copy(s).wait()
+
+    for k in range(reflections_n):
+        slot = inverse_ref[k * FRAMES + lax.rem(group + k, FRAMES)]
+        seen = images[lax.rem(me - slot + n, n)].astype(jnp.float32)
+        gathered[0, k] = (seen - total[k]).astype(jnp.bfloat16)
+
+    def gather_copy(s):
+        other = lax.rem(member + s, members)
+        return remote(
+            gathered.at[0], gathered.at[s], gather_send.at[s - 1], gather_recv.at[s - 1],
+            other * FRAMES + group,
+        )
+
+    for s in range(1, members):
+        gather_copy(s).start()
+    for s in range(1, members):
+        gather_copy(s).wait()
+
+    def quad_copy(s):
+        other = lax.rem(group + s, FRAMES)
+        return remote(
+            outgoing.at[s - 1], incoming.at[s], quad_send.at[s - 1], quad_recv.at[s - 1],
+            member * FRAMES + other,
+        )
+
+    for s in range(FRAMES):
+        wanted = slot_ref[member * FRAMES + lax.rem(group + s, FRAMES)] // FRAMES
+        for i in range(members):
+            block = gathered[i, wanted]
+            if s == 0:
+                incoming[0, i] = block
+            else:
+                outgoing[s - 1, i] = block
+        if s:
+            quad_copy(s).start()
+    for k in range(reflections_n):
+        inside = band(start_ref, len_ref, k, (share, detector))
+        for i in range(members):
+            owner = lax.rem(member - i + members, members)
+            rows = pl.ds(pl.multiple_of(owner * share, share), share)
+            masked_ref[rows, k * detector:(k + 1) * detector] = jnp.where(
+                inside, gathered[i, k].astype(jnp.float32), 0.0
+            ).astype(jnp.bfloat16)
+    for s in range(1, FRAMES):
+        quad_copy(s).wait()
+    mine = slot_ref[me]
+    held = lax.rem(lax.rem(mine, FRAMES) - lax.rem(mine // FRAMES, FRAMES) + FRAMES, FRAMES)
+    back = lax.rem(group - held + FRAMES, FRAMES)
+    for i in range(members):
+        owner = lax.rem(member - i + members, members)
+        rows = pl.ds(pl.multiple_of(owner * share, share), share)
+        residual_ref[rows, :] = incoming[back, i].astype(jnp.float32)
+
+
+def backward_kernel(scale_ref, volume_ref, flat_ref, masked_ref, updated_ref):
+    gradient = lax.dot_general(
+        masked_ref[...], flat_ref[...], (((1,), (1,)), ((), ())), preferred_element_type=jnp.float32
+    )
+    density = volume_ref[...].astype(jnp.float32) + scale_ref[0] * gradient
+    edge = jnp.zeros_like(density[:1])
+    for repeat in range(SWEEPS):
+        flux = jnp.clip(density[1:] - density[:-1], -huber_delta, huber_delta)
+        above = jnp.concatenate([edge, flux], axis=0)
+        below = jnp.concatenate([flux, edge], axis=0)
+        density = density - sweep_rate * (above - below)
+    updated_ref[...] = density.astype(jnp.bfloat16)
+
+
+def fast(volume, rays, band_start, band_len, slot_image, measured, relax):
+    _, rows, cell_count = volume.shape
+    _, reflections_n, detector = rays.shape
+    n = lax.axis_size("orient")
+    members = n // FRAMES
+    share = rows // members
+    images_n = slot_image.shape[0]
+    wide_n = reflections_n * detector
+    tile = min(512, cell_count)
+    volume = volume.reshape(rows, cell_count)
+    smem = pl.BlockSpec(memory_space=pltpu.SMEM)
+    vmem = pl.BlockSpec(memory_space=pltpu.VMEM)
+    flat, contrib = pl.pallas_call(
+        forward_kernel,
+        grid=(cell_count // tile,),
+        in_specs=[
+            smem,
+            smem,
+            pl.BlockSpec((rows, tile), lambda c: (0, c)),
+            pl.BlockSpec((tile, reflections_n, detector), lambda c: (c, 0, 0)),
+        ],
+        out_specs=[
+            pl.BlockSpec((tile, wide_n), lambda c: (c, 0)),
+            pl.BlockSpec((members, reflections_n, share, detector), lambda c: (0, 0, 0, 0)),
+        ],
+        out_shape=[
+            jax.ShapeDtypeStruct((cell_count, wide_n), jnp.bfloat16),
+            jax.ShapeDtypeStruct((members, reflections_n, share, detector), jnp.bfloat16),
+        ],
+        scratch_shapes=[
+            pltpu.VMEM((tile * reflections_n, detector), jnp.float32),
+            pltpu.VMEM((rows, wide_n), jnp.float32),
+        ],
+        compiler_params=pltpu.CompilerParams(vmem_limit_bytes=32 * 2**20),
+        name="forward",
+    )(band_start, band_len, volume, rays)
+    inverse = jnp.sum(
+        jnp.where(
+            slot_image[None, :] == jnp.arange(images_n, dtype=jnp.int32)[:, None],
+            jnp.arange(images_n, dtype=jnp.int32)[None, :],
+            0,
+        ),
+        axis=1,
+    )
+    narrow = measured.astype(jnp.bfloat16).reshape(members, share, detector)
+    block = (reflections_n, share, detector)
+    masked, residual = pl.pallas_call(
+        lambda *refs: exchange_kernel(n, *refs),
+        in_specs=[smem, smem, smem, smem, vmem, vmem],
+        out_specs=[vmem, vmem],
+        out_shape=[
+            jax.ShapeDtypeStruct((rows, wide_n), jnp.bfloat16),
+            jax.ShapeDtypeStruct((rows, detector), jnp.float32),
+        ],
+        scratch_shapes=[
+            pltpu.VMEM((members - 1,) + block, jnp.bfloat16),
+            pltpu.VMEM((n, share, detector), jnp.bfloat16),
+            pltpu.VMEM((members,) + block, jnp.bfloat16),
+            pltpu.VMEM((FRAMES - 1, members, share, detector), jnp.bfloat16),
+            pltpu.VMEM((FRAMES, members, share, detector), jnp.bfloat16),
+            pltpu.SemaphoreType.DMA((n,)),
+            pltpu.SemaphoreType.DMA((n,)),
+            pltpu.SemaphoreType.DMA((members - 1,)),
+            pltpu.SemaphoreType.DMA((members - 1,)),
+            pltpu.SemaphoreType.DMA((members - 1,)),
+            pltpu.SemaphoreType.DMA((members - 1,)),
+            pltpu.SemaphoreType.DMA((FRAMES - 1,)),
+            pltpu.SemaphoreType.DMA((FRAMES - 1,)),
+        ],
+        compiler_params=pltpu.CompilerParams(
+            collective_id=0, has_side_effects=True, vmem_limit_bytes=16 * 2**20
+        ),
+        name="exchange",
+    )(band_start, band_len, slot_image, inverse, contrib, narrow)
+    step_gain = math.sqrt(cell_count * n / (FRAMES * reflections_n * detector))
+    updated = pl.pallas_call(
+        backward_kernel,
+        grid=(cell_count // tile,),
+        in_specs=[
+            smem,
+            pl.BlockSpec((rows, tile), lambda c: (0, c)),
+            pl.BlockSpec((tile, wide_n), lambda c: (c, 0)),
+            pl.BlockSpec((rows, wide_n), lambda c: (0, 0)),
+        ],
+        out_specs=pl.BlockSpec((rows, tile), lambda c: (0, c)),
+        out_shape=jax.ShapeDtypeStruct((rows, cell_count), jnp.bfloat16),
+        compiler_params=pltpu.CompilerParams(vmem_limit_bytes=32 * 2**20),
+        name="backward",
+    )(relax * step_gain, volume, flat, masked)
+    return updated[None], residual[None]
+
+
+def chosen(*operands):
+    volume, rays, _, _, slot_image, measured, _ = operands
+    n = lax.axis_size("orient")
+    plain = (
+        lax.axis_size("slab") == 1
+        and volume.shape[0] == 1
+        and measured.shape[0] == 1
+        and n % FRAMES == 0
+        and n > FRAMES
+        and volume.shape[1] % (16 * (n // FRAMES)) == 0
+        and volume.shape[2] % min(512, volume.shape[2]) == 0
+        and rays.shape[1] % 8 == 0
+        and rays.shape[2] % 128 == 0
+    )
+    return fast(*operands) if plain else local(*operands)
+
+
 def solution(mesh):
     placed = (
         P("orient", "slab", None),
@@ -100,7 +365,7 @@
         P("orient"),
     )
     return jax.shard_map(
-        local,
+        chosen,
         mesh=mesh,
         in_specs=placed,
         out_specs=(P("orient", "slab", None), P("orient", "slab", None)),

time: 255 us -> 76.6 us (0.30); the launches traced: 251 us -> 76 us
  other arithmetic: 88.2 us -> 1.61 us
  local copies, waits for them, and re-layouts: 85 us -> 15.2 us
  Pallas kernels: 0 us -> 57.9 us
  waiting for transfers between devices: 32.5 us -> 0 us
  starting transfers between devices: 22.1 us -> 0 us
  matrix products: 21.9 us -> 0 us
    unnamed x2 -> x0, other arithmetic: 75.3 us -> none
    pallas_call x0 -> x3, Pallas kernels: none -> 57.9 us  [the longest x1 28.2 us: fast(): pl.pallas_call(lambda *refs: exchange_kernel(n, *refs), in_specs=[smem, s...]
    all_to_all x4 -> x0, waiting for transfers between devices: 32.5 us -> none  [the longest x1 13.3 us: local(): lax.all_to_all(contrib, 'orient', split_axis=2, concat_axis=0, tiled=True)]
    unnamed x18 -> x13, local copies, waits for them, and re-layouts: 40.1 us -> 15.2 us
    dot_general x3 -> x0, matrix products: 21.9 us -> none  [the longest x1 13.4 us: local(): jnp.einsum('okrd,ckd->orc', masked, rays, preferred_element_type=jnp.floa...]
    dot_general x1 -> x0, local copies, waits for them, and re-layouts: 21.5 us -> none  [local(): jnp.dot(volume.reshape(or_dev * row_dev, cell_count), flat_rays, preferre...]
    all_to_all x4 -> x0, starting transfers between devices: 19.3 us -> none  [the longest x1 6.36 us: local(): lax.all_to_all(contrib, 'orient', split_axis=2, concat_axis=0, tiled=True)]
    reshape x3 -> x0, local copies, waits for them, and re-layouts: 12.1 us -> none  [the longest x1 11.9 us: local(): jnp.einsum('kod,orkd->okrd', band_mask, projected)]
  transfers between devices with their start and end apart: 8 -> 0, of which waited for: 4 -> 0; matrix products, arithmetic and copies ran while one was open for 0% -> 0% of each run, Pallas kernels for 0% -> 0%
where the time goes in v1:
time: 76.6 us; the launch traced here: 76 us
  Pallas kernels  57.9 us (76%)
  local copies, waits for them, and re-layouts  15.2 us (20%)
  other arithmetic  1.61 us (2%)
  between operations  1.34 us (2%)
    pallas_call x1, Pallas kernels, fast(): pl.pallas_call(lambda *refs: exchange_kernel(n, *refs), in_specs=[smem, s...  28.2 us
    pallas_call x1, Pallas kernels, fast(): pl.pallas_call(forward_kernel, grid=(cell_count // tile,), in_specs=[smem...  18.1 us
    unnamed x13, local copies, waits for them, and re-layouts  15.2 us
    pallas_call x1, Pallas kernels, fast(): pl.pallas_call(backward_kernel, grid=(cell_count // tile,), in_specs=[sme...  11.6 us

profile of v1, /device:TPU:9, one launch (start us, length us, event | category | flops | bytes accessed | tf_op | source)
XLA Modules:
  0.0 76.0 jit_solution(6865041161831691444)
XLA Ops:
  0.6 0.0 copy-start.4
  1.3 0.8 %select_reduce_fusion.refs_3_ = s32[32]{0:T(128)S(1)} fusion(s32[32]{0:T(128)} %refs_2_.1), kind=kLoop, calls=%fused_computation | loop fusion | flops 3040 | bytes 256 | tf_op jit(solution)/shard_map/reduce_sum | solution.py:284
  2.1 0.7 copy.13.start_ref.refs_0_
  2.8 0.7 copy.14.len_ref.refs_1_
  3.5 0.8 %convert_element_type.3 = bf16[1,128,128]{2,1,0:T(8,128)(2,1)S(1)} convert(f32[1,128,128]{2,1,0:T(8,128)} %param.12) | non-fusion elementwise | flops 16384 | bytes 98304 | tf_op jit(solution)/shard_map/convert_element_type | solution.py:292
  4.4 0.0 copy-start.2
  4.4 1.6 %copy-done.2 = bf16[1,128,8192]{2,1,0:T(8,128)(2,1)S(1)} copy-done((bf16[1,128,8192]{2,1,0:T(8,128)(2,1)S(1)}, bf16[1,128,8192]{2,1,0:T(8,128)(2,1)}, u32[]{:S(2)}) %copy-start.2) | copy-done | bytes 2097176
  6.0 0.0 copy-start.3
  6.0 18.1 %forward.1 = (bf16[8192,1024]{1,0:T(8,128)(2,1)S(1)}, bf16[8,8,16,128]{3,2,1,0:T(8,128)(2,1)S(1)}) custom-call(s32[8,1]{1,0:T(8,128)S(1)} %copy.13.start_ref.refs_0_, s32[8,1]{1,0:T(8,128)S(1)} %copy.14.len_ref.refs_1_, bf16[128,8192]{1,0:T(8,128)(2,1)S(1)} %bitcast.4, bf16[8192,8,128]{2,1,0:T(8,128)(2,1)} %rays_ref.1), custom_call_target="tpu_custom_call" | custom-call | tf_op jit(solution)/shard_map/forward/pallas_call | solution.py:260
  24.0 0.0 copy-start
  24.0 5.7 %copy-done = bf16[8192,1024]{1,0:T(8,128)(2,1)} copy-done((bf16[8192,1024]{1,0:T(8,128)(2,1)}, bf16[8192,1024]{1,0:T(8,128)(2,1)S(1)}, u32[]{:S(2)}) %copy-start) | copy-done | bytes 16777240
  29.8 0.0 copy-done.4
  29.8 28.2 %exchange.1 = (bf16[128,1024]{1,0:T(8,128)(2,1)S(1)}, f32[128,128]{1,0:T(8,128)S(1)}) custom-call(s32[8,1]{1,0:T(8,128)S(1)} %copy.13.start_ref.refs_0_, s32[8,1]{1,0:T(8,128)S(1)} %copy.14.len_ref.refs_1_, s32[32]{0:T(128)S(1)} %copy-done.4, s32[32]{0:T(128)S(1)} %select_reduce_fusion.refs_3_, bf16[8,8,16,128]{3,2,1,0:T(8,128)(2,1)S(1)} %get-tuple-element.7.refs_4_, ...), custom_call_target="tpu_custom_call" | custom-call | tf_op jit(solution)/shard_map/exchange/pallas_call | solution.py:294
  58.0 0.0 copy-done.3
  58.0 0.0 copy-start.1
  58.0 5.8 %copy-done.1 = bf16[8192,1024]{1,0:T(8,128)(2,1)S(1)} copy-done((bf16[8192,1024]{1,0:T(8,128)(2,1)S(1)}, bf16[8192,1024]{1,0:T(8,128)(2,1)}, u32[]{:S(2)}) %copy-start.1) | copy-done | bytes 16777240
  63.8 11.6 %backward.1 = bf16[128,8192]{1,0:T(8,128)(2,1)} custom-call(f32[1]{0:T(128)S(6)} %mul.3.scale_ref, bf16[128,8192]{1,0:T(8,128)(2,1)S(1)} %bitcast.5, bf16[8192,1024]{1,0:T(8,128)(2,1)S(1)} %copy-done.1, bf16[128,1024]{1,0:T(8,128)(2,1)S(1)} %get-tuple-element.8.masked_ref), custom_call_target="tpu_custom_call" | custom-call | tf_op jit(solution)/shard_map/backward/pallas_call | solution.py:323
  75.4 0.6 copy.19
Async XLA Ops:
  0.6 29.1 %copy-start.4 = (s32[32]{0:T(128)S(1)}, s32[32]{0:T(128)}, u32[]{:S(2)}) copy-start(s32[32]{0:T(128)} %refs_2_.1) | copy-start | bytes 388
  4.4 1.6 %copy-start.2 = (bf16[1,128,8192]{2,1,0:T(8,128)(2,1)S(1)}, bf16[1,128,8192]{2,1,0:T(8,128)(2,1)}, u32[]{:S(2)}) copy-start(bf16[1,128,8192]{2,1,0:T(8,128)(2,1)} %param.7) | copy-start | bytes 6291460
  6.0 52.0 %copy-start.3 = (bf16[1,128,8192]{2,1,0:T(8,128)(2,1)S(1)}, bf16[1,128,8192]{2,1,0:T(8,128)(2,1)}, u32[]{:S(2)}) copy-start(bf16[1,128,8192]{2,1,0:T(8,128)(2,1)} %param.7) | copy-start | bytes 6291460
  24.0 5.7 %copy-start = (bf16[8192,1024]{1,0:T(8,128)(2,1)}, bf16[8192,1024]{1,0:T(8,128)(2,1)S(1)}, u32[]{:S(2)}) copy-start(bf16[8192,1024]{1,0:T(8,128)(2,1)S(1)} %get-tuple-element.6.flat_ref) | copy-start | bytes 50331652
  58.0 5.8 %copy-start.1 = (bf16[8192,1024]{1,0:T(8,128)(2,1)S(1)}, bf16[8192,1024]{1,0:T(8,128)(2,1)}, u32[]{:S(2)}) copy-start(bf16[8192,1024]{1,0:T(8,128)(2,1)} %copy-done) | copy-start | bytes 50331652

commit v2 on v1

--- a/solution.py
+++ b/solution.py
@@ -1,3 +1,4 @@
+import functools
 import math
 
 import jax
@@ -122,8 +123,8 @@
 
 
 def exchange_kernel(
-    n, start_ref, len_ref, slot_ref, inverse_ref, contrib_ref, measured_ref, masked_ref, residual_ref,
-    pieces, images, gathered, outgoing, incoming,
+    n, start_ref, len_ref, slot_ref, contrib_ref, measured_ref, masked_ref, residual_ref,
+    narrow, pieces, images, gathered, outgoing, incoming,
     image_send, image_recv, piece_send, piece_recv, gather_send, gather_recv, quad_send, quad_recv,
 ):
     members, reflections_n, share, detector = contrib_ref.shape
@@ -146,6 +147,7 @@
             device_id_type=pl.DeviceIdType.MESH,
         )
 
+    narrow[...] = measured_ref[...].astype(jnp.bfloat16)
     pl.semaphore_wait(barrier, n - 1)
 
     def piece_copy(s):
@@ -158,7 +160,7 @@
     def image_copy(s):
         device = lax.rem(me + s, n)
         return remote(
-            measured_ref.at[device // FRAMES], images.at[s], image_send.at[s], image_recv.at[s], device
+            narrow.at[device // FRAMES], images.at[s], image_send.at[s], image_recv.at[s], device
         )
 
     for s in range(1, members):
@@ -168,7 +170,7 @@
     def _(s):
         image_copy(s).start()
 
-    images[0] = measured_ref[member]
+    images[0] = narrow[member]
     total = contrib_ref[member].astype(jnp.float32)
     for s in range(1, members):
         piece_copy(s).wait()
@@ -179,7 +181,10 @@
         image_copy(s).wait()
 
     for k in range(reflections_n):
-        slot = inverse_ref[k * FRAMES + lax.rem(group + k, FRAMES)]
+        image = k * FRAMES + lax.rem(group + k, FRAMES)
+        slot = jnp.int32(0)
+        for j in range(slot_ref.shape[0]):
+            slot = jnp.where(slot_ref[j] == image, j, slot)
         seen = images[lax.rem(me - slot + n, n)].astype(jnp.float32)
         gathered[0, k] = (seen - total[k]).astype(jnp.bfloat16)
 
@@ -231,11 +236,11 @@
         residual_ref[rows, :] = incoming[back, i].astype(jnp.float32)
 
 
-def backward_kernel(scale_ref, volume_ref, flat_ref, masked_ref, updated_ref):
+def backward_kernel(step_gain, relax_ref, volume_ref, flat_ref, masked_ref, updated_ref):
     gradient = lax.dot_general(
         masked_ref[...], flat_ref[...], (((1,), (1,)), ((), ())), preferred_element_type=jnp.float32
     )
-    density = volume_ref[...].astype(jnp.float32) + scale_ref[0] * gradient
+    density = volume_ref[...].astype(jnp.float32) + relax_ref[0] * step_gain * gradient
     edge = jnp.zeros_like(density[:1])
     for repeat in range(SWEEPS):
         flux = jnp.clip(density[1:] - density[:-1], -huber_delta, huber_delta)
@@ -278,28 +283,20 @@
             pltpu.VMEM((tile * reflections_n, detector), jnp.float32),
             pltpu.VMEM((rows, wide_n), jnp.float32),
         ],
-        compiler_params=pltpu.CompilerParams(vmem_limit_bytes=32 * 2**20),
+        compiler_params=pltpu.CompilerParams(vmem_limit_bytes=60 * 2**20),
         name="forward",
     )(band_start, band_len, volume, rays)
-    inverse = jnp.sum(
-        jnp.where(
-            slot_image[None, :] == jnp.arange(images_n, dtype=jnp.int32)[:, None],
-            jnp.arange(images_n, dtype=jnp.int32)[None, :],
-            0,
-        ),
-        axis=1,
-    )
-    narrow = measured.astype(jnp.bfloat16).reshape(members, share, detector)
     block = (reflections_n, share, detector)
     masked, residual = pl.pallas_call(
         lambda *refs: exchange_kernel(n, *refs),
-        in_specs=[smem, smem, smem, smem, vmem, vmem],
+        in_specs=[smem, smem, smem, vmem, vmem],
         out_specs=[vmem, vmem],
         out_shape=[
             jax.ShapeDtypeStruct((rows, wide_n), jnp.bfloat16),
             jax.ShapeDtypeStruct((rows, detector), jnp.float32),
         ],
         scratch_shapes=[
+            pltpu.VMEM((members, share, detector), jnp.bfloat16),
             pltpu.VMEM((members - 1,) + block, jnp.bfloat16),
             pltpu.VMEM((n, share, detector), jnp.bfloat16),
             pltpu.VMEM((members,) + block, jnp.bfloat16),
@@ -315,13 +312,13 @@
             pltpu.SemaphoreType.DMA((FRAMES - 1,)),
         ],
         compiler_params=pltpu.CompilerParams(
-            collective_id=0, has_side_effects=True, vmem_limit_bytes=16 * 2**20
+            collective_id=0, has_side_effects=True, vmem_limit_bytes=60 * 2**20
         ),
         name="exchange",
-    )(band_start, band_len, slot_image, inverse, contrib, narrow)
+    )(band_start, band_len, slot_image, contrib, measured.reshape(members, share, detector))
     step_gain = math.sqrt(cell_count * n / (FRAMES * reflections_n * detector))
     updated = pl.pallas_call(
-        backward_kernel,
+        functools.partial(backward_kernel, step_gain),
         grid=(cell_count // tile,),
         in_specs=[
             smem,
@@ -331,9 +328,9 @@
         ],
         out_specs=pl.BlockSpec((rows, tile), lambda c: (0, c)),
         out_shape=jax.ShapeDtypeStruct((rows, cell_count), jnp.bfloat16),
-        compiler_params=pltpu.CompilerParams(vmem_limit_bytes=32 * 2**20),
+        compiler_params=pltpu.CompilerParams(vmem_limit_bytes=60 * 2**20),
         name="backward",
-    )(relax * step_gain, volume, flat, masked)
+    )(relax, volume, flat, masked)
     return updated[None], residual[None]
 
 

time: 76.6 us -> 75 us (0.979)
  local copies, waits for them, and re-layouts: 15.2 us -> 3.26 us
  Pallas kernels: 57.9 us -> 69.3 us
  other arithmetic: 1.61 us -> 0 us
    unnamed x13 -> x5, local copies, waits for them, and re-layouts: 15.2 us -> 3.26 us
    pallas_call x1, Pallas kernels: 11.6 us -> 18 us  [fast(): pl.pallas_call(functools.partial(backward_kernel, step_gain), grid=(cell_...]
    pallas_call x1, Pallas kernels: 18.1 us -> 21.9 us  [fast(): pl.pallas_call(forward_kernel, grid=(cell_count // tile,), in_specs=[smem...]
    pallas_call x1, Pallas kernels: 28.2 us -> 29.4 us  [fast(): pl.pallas_call(lambda *refs: exchange_kernel(n, *refs), in_specs=[smem, s...]
    convert_element_type x1 -> x0, other arithmetic: 0.84 us -> none  [fast(): narrow = measured.astype(jnp.bfloat16).reshape(members, share, detector)]
    reduce_sum x1 -> x0, other arithmetic: 0.77 us -> none  [fast(): jnp.sum(jnp.where(slot_image[None, :] == jnp.arange(images_n, dtype=jnp.i...]
where the time goes in v2:
time: 75 us; the launch traced here: 73.9 us
  Pallas kernels  69.3 us (92%)
  local copies, waits for them, and re-layouts  3.26 us (4%)
  between operations  1.3 us (2%)
    pallas_call x1, Pallas kernels, fast(): pl.pallas_call(lambda *refs: exchange_kernel(n, *refs), in_specs=[smem, s...  29.4 us
    pallas_call x1, Pallas kernels, fast(): pl.pallas_call(forward_kernel, grid=(cell_count // tile,), in_specs=[smem...  21.9 us
    pallas_call x1, Pallas kernels, fast(): pl.pallas_call(functools.partial(backward_kernel, step_gain), grid=(cell_...  18 us
    unnamed x5, local copies, waits for them, and re-layouts  3.26 us

profile of v2, /device:TPU:9, one launch (start us, length us, event | category | flops | bytes accessed | tf_op | source)
XLA Modules:
  0.0 73.9 jit_solution(10352752353082807991)
XLA Ops:
  1.3 1.3 %copy.9.start_ref.refs_0_ = s32[8,1]{1,0:T(8,128)} copy(s32[8,1]{0,1:T(1,128)} %param.9) | data formatting | bytes 64 | tf_op args[2]
  2.6 1.3 %copy.10.len_ref.refs_1_ = s32[8,1]{1,0:T(8,128)} copy(s32[8,1]{0,1:T(1,128)} %param.10) | data formatting | bytes 64 | tf_op args[3]
  3.9 21.9 %forward.1 = (bf16[8192,1024]{1,0:T(8,128)(2,1)}, bf16[8,8,16,128]{3,2,1,0:T(8,128)(2,1)}) custom-call(s32[8,1]{1,0:T(8,128)} %copy.9.start_ref.refs_0_, s32[8,1]{1,0:T(8,128)} %copy.10.len_ref.refs_1_, bf16[128,8192]{1,0:T(8,128)(2,1)} %bitcast.4, bf16[8192,8,128]{2,1,0:T(8,128)(2,1)} %rays_ref.1), custom_call_target="tpu_custom_call" | custom-call | tf_op jit(solution)/shard_map/forward/pallas_call | solution.py:265
  25.9 29.4 %exchange.1 = (bf16[128,1024]{1,0:T(8,128)(2,1)}, f32[128,128]{1,0:T(8,128)}) custom-call(s32[8,1]{1,0:T(8,128)} %copy.9.start_ref.refs_0_, s32[8,1]{1,0:T(8,128)} %copy.10.len_ref.refs_1_, s32[32]{0:T(128)} %refs_2_.1, bf16[8,8,16,128]{3,2,1,0:T(8,128)(2,1)} %get-tuple-element.7.refs_3_, f32[8,16,128]{2,1,0:T(8,128)} %bitcast.8), custom_call_target="tpu_custom_call" | custom-call | tf_op jit(solution)/shard_map/exchange/pallas_call | solution.py:290
  55.3 0.0 copy-start
  55.3 18.0 %backward.1 = bf16[128,8192]{1,0:T(8,128)(2,1)} custom-call(f32[1]{0:T(128)S(6)} %copy.14.relax_ref, bf16[128,8192]{1,0:T(8,128)(2,1)} %bitcast.5, bf16[8192,1024]{1,0:T(8,128)(2,1)} %get-tuple-element.6.flat_ref, bf16[128,1024]{1,0:T(8,128)(2,1)} %get-tuple-element.8.masked_ref), custom_call_target="tpu_custom_call" | custom-call | tf_op jit(solution)/shard_map/backward/pallas_call | solution.py:320
  73.3 0.0 copy-done
  73.3 0.6 copy.15
Async XLA Ops:
  55.3 18.0 %copy-start = (f32[128,128]{1,0:T(8,128)S(1)}, f32[128,128]{1,0:T(8,128)}, u32[]{:S(2)}) copy-start(f32[128,128]{1,0:T(8,128)} %get-tuple-element.9) | copy-start | bytes 196612

commit v3 on v2

--- a/solution.py
+++ b/solution.py
@@ -283,7 +283,7 @@
             pltpu.VMEM((tile * reflections_n, detector), jnp.float32),
             pltpu.VMEM((rows, wide_n), jnp.float32),
         ],
-        compiler_params=pltpu.CompilerParams(vmem_limit_bytes=60 * 2**20),
+        compiler_params=pltpu.CompilerParams(vmem_limit_bytes=12 * 2**20),
         name="forward",
     )(band_start, band_len, volume, rays)
     block = (reflections_n, share, detector)
@@ -312,7 +312,7 @@
             pltpu.SemaphoreType.DMA((FRAMES - 1,)),
         ],
         compiler_params=pltpu.CompilerParams(
-            collective_id=0, has_side_effects=True, vmem_limit_bytes=60 * 2**20
+            collective_id=0, has_side_effects=True, vmem_limit_bytes=4 * 2**20
         ),
         name="exchange",
     )(band_start, band_len, slot_image, contrib, measured.reshape(members, share, detector))
@@ -328,7 +328,7 @@
         ],
         out_specs=pl.BlockSpec((rows, tile), lambda c: (0, c)),
         out_shape=jax.ShapeDtypeStruct((rows, cell_count), jnp.bfloat16),
-        compiler_params=pltpu.CompilerParams(vmem_limit_bytes=60 * 2**20),
+        compiler_params=pltpu.CompilerParams(vmem_limit_bytes=12 * 2**20),
         name="backward",
     )(relax, volume, flat, masked)
     return updated[None], residual[None]

time: 75 us -> 65.1 us (0.87); the launches traced: 73.9 us -> 64.9 us
  Pallas kernels: 69.3 us -> 54.1 us
  local copies, waits for them, and re-layouts: 3.26 us -> 9.46 us
    pallas_call x1, Pallas kernels: 21.9 us -> 14.1 us  [fast(): pl.pallas_call(forward_kernel, grid=(cell_count // tile,), in_specs=[smem...]
    pallas_call x1, Pallas kernels: 18 us -> 11.6 us  [fast(): pl.pallas_call(functools.partial(backward_kernel, step_gain), grid=(cell_...]
    unnamed x5 -> x11, local copies, waits for them, and re-layouts: 3.26 us -> 9.46 us
    pallas_call x1, Pallas kernels: 29.4 us -> 28.4 us  [fast(): pl.pallas_call(lambda *refs: exchange_kernel(n, *refs), in_specs=[smem, s...]
where the time goes in v3:
time: 65.1 us; the launch traced here: 64.9 us
  Pallas kernels  54.1 us (83%)
  local copies, waits for them, and re-layouts  9.46 us (15%)
  between operations  1.33 us (2%)
    pallas_call x1, Pallas kernels, fast(): pl.pallas_call(lambda *refs: exchange_kernel(n, *refs), in_specs=[smem, s...  28.4 us
    pallas_call x1, Pallas kernels, fast(): pl.pallas_call(forward_kernel, grid=(cell_count // tile,), in_specs=[smem...  14.1 us
    pallas_call x1, Pallas kernels, fast(): pl.pallas_call(functools.partial(backward_kernel, step_gain), grid=(cell_...  11.6 us
    unnamed x11, local copies, waits for them, and re-layouts  9.46 us

profile of v3, /device:TPU:9, one launch (start us, length us, event | category | flops | bytes accessed | tf_op | source)
XLA Modules:
  0.0 64.9 jit_solution(14110351311388374264)
XLA Ops:
  0.6 0.0 copy-start.3
  1.3 0.7 %copy.9.start_ref.refs_0_ = s32[8,1]{1,0:T(8,128)S(1)} copy(s32[8,1]{0,1:T(1,128)} %param.9) | data formatting | bytes 64 | tf_op args[2]
  2.0 0.7 %copy.10.len_ref.refs_1_ = s32[8,1]{1,0:T(8,128)S(1)} copy(s32[8,1]{0,1:T(1,128)} %param.10) | data formatting | bytes 64 | tf_op args[3]
  2.8 0.0 copy-start
  2.8 5.8 %copy-done = bf16[8192,8,128]{2,1,0:T(8,128)(2,1)S(1)} copy-done((bf16[8192,8,128]{2,1,0:T(8,128)(2,1)S(1)}, bf16[8192,8,128]{2,1,0:T(8,128)(2,1)}, u32[]{:S(2)}) %copy-start) | copy-done | bytes 16777240
  8.5 0.0 copy-start.1
  8.5 1.6 %copy-done.1 = bf16[1,128,8192]{2,1,0:T(8,128)(2,1)S(1)} copy-done((bf16[1,128,8192]{2,1,0:T(8,128)(2,1)S(1)}, bf16[1,128,8192]{2,1,0:T(8,128)(2,1)}, u32[]{:S(2)}) %copy-start.1) | copy-done | bytes 2097176
  10.1 0.0 copy-start.2
  10.1 14.1 %forward.1 = (bf16[8192,1024]{1,0:T(8,128)(2,1)S(1)}, bf16[8,8,16,128]{3,2,1,0:T(8,128)(2,1)S(1)}) custom-call(s32[8,1]{1,0:T(8,128)S(1)} %copy.9.start_ref.refs_0_, s32[8,1]{1,0:T(8,128)S(1)} %copy.10.len_ref.refs_1_, bf16[128,8192]{1,0:T(8,128)(2,1)S(1)} %bitcast.4, bf16[8192,8,128]{2,1,0:T(8,128)(2,1)S(1)} %copy-done), custom_call_target="tpu_custom_call" | custom-call | tf_op jit(solution)/shard_map/forward/pallas_call | solution.py:265
  24.2 0.0 copy-done.3
  24.2 0.0 copy-done.2
  24.2 28.4 %exchange.1 = (bf16[128,1024]{1,0:T(8,128)(2,1)S(1)}, f32[128,128]{1,0:T(8,128)S(1)}) custom-call(s32[8,1]{1,0:T(8,128)S(1)} %copy.9.start_ref.refs_0_, s32[8,1]{1,0:T(8,128)S(1)} %copy.10.len_ref.refs_1_, s32[32]{0:T(128)S(1)} %copy-done.3, bf16[8,8,16,128]{3,2,1,0:T(8,128)(2,1)S(1)} %get-tuple-element.7.refs_3_, f32[8,16,128]{2,1,0:T(8,128)S(1)} %bitcast.7), custom_call_target="tpu_custom_call" | custom-call | tf_op jit(solution)/shard_map/exchange/pallas_call | solution.py:290
  52.6 11.6 %backward.1 = bf16[128,8192]{1,0:T(8,128)(2,1)} custom-call(f32[1]{0:T(128)S(6)} %copy.14.relax_ref, bf16[128,8192]{1,0:T(8,128)(2,1)S(1)} %bitcast.5, bf16[8192,1024]{1,0:T(8,128)(2,1)S(1)} %get-tuple-element.6.flat_ref, bf16[128,1024]{1,0:T(8,128)(2,1)S(1)} %get-tuple-element.8.masked_ref), custom_call_target="tpu_custom_call" | custom-call | tf_op jit(solution)/shard_map/backward/pallas_call | solution.py:320
  64.2 0.6 copy.15
Async XLA Ops:
  0.6 23.6 %copy-start.3 = (s32[32]{0:T(128)S(1)}, s32[32]{0:T(128)}, u32[]{:S(2)}) copy-start(s32[32]{0:T(128)} %refs_2_.1) | copy-start | bytes 388
  2.8 5.8 %copy-start = (bf16[8192,8,128]{2,1,0:T(8,128)(2,1)S(1)}, bf16[8192,8,128]{2,1,0:T(8,128)(2,1)}, u32[]{:S(2)}) copy-start(bf16[8192,8,128]{2,1,0:T(8,128)(2,1)} %rays_ref.1) | copy-start | bytes 50331652
  8.5 1.6 %copy-start.1 = (bf16[1,128,8192]{2,1,0:T(8,128)(2,1)S(1)}, bf16[1,128,8192]{2,1,0:T(8,128)(2,1)}, u32[]{:S(2)}) copy-start(bf16[1,128,8192]{2,1,0:T(8,128)(2,1)} %param.7) | copy-start | bytes 6291460
  10.1 14.1 %copy-start.2 = (f32[1,128,128]{2,1,0:T(8,128)S(1)}, f32[1,128,128]{2,1,0:T(8,128)}, u32[]{:S(2)}) copy-start(f32[1,128,128]{2,1,0:T(8,128)} %param.12) | copy-start | bytes 196612
